TPU v7x, 128 devices: a whole 4x4x4 slice. The times are simulated.
128 devices in a mesh: grp: 8 (over x, core), soil: 16 (over z, y).
Axes of the slice: x: 4, y: 4, z: 4, core: 2. Of those that a mesh axis runs over, the one named last changes fastest.
Arguments:
- warm_start: float32 [3, 131072], P(None, ('grp', 'soil')), may hold values from -5 to 5
- right_side: float32 [3, 131072], P(None, ('grp', 'soil')), may hold values from -16 to 16
- friction: float32 [131072], P(('grp', 'soil')), may hold values from 0.3 to 1
- inverse_mass: float32 [6, 131072], P(None, ('grp', 'soil')), may hold values from 0.5 to 2
- jacobian: bfloat16 [8192, 192, 384], P(('grp', 'soil')), may hold values from -0.15625 to 0.15625
- compliance: bfloat16 [6144, 6144], P(None, 'soil'), may hold values from -0.5 to 2.5, as said below
- entry_block: int32 [8192], P(('grp', 'soil')), may hold values from 0 to 15
- entry_owner: int32 [8192], P(('grp', 'soil')), may hold values from 0 to 15, as said below
- entry_body: int32 [8192], P(('grp', 'soil')), may hold values from 0 to 15
- block_count: int32 [128], P(('grp', 'soil')), may hold values from 16 to 64, as said below
Outputs:
- impulses: float32 [3, 131072], P(None, ('grp', 'soil'))
- velocity_change: float32 [6, 131072], P(None, ('grp', 'soil'))
- change_norm: float32 [], replicated
Inputs may be any that keep to these rules, and one draw needn't show every extreme that they name: `entry_owner`: among the first block_count entries of a device at most 4 name one owner, and one owner of every group receives 4 entries from each of the 16 devices of that group; later entries are padding. `block_count`: one device of every group holds 64 live entries; the others hold 16 to 32. `compliance`: Symmetric.
All inputs are finite; a program needn't handle non-finite values.
Results may differ from a plain program's by a relative error of at most 0.0032.
Values may be sent and summed in bfloat16 or wider, within the bound.
No kernel may reach another device: no remote copies, remote signals or barrier semaphores. Data moves between devices by JAX's collectives and lax.ppermute only.
A program may use at most 64 MiB of HBM per device.

v0:
```python
import functools
import math

import jax
import jax.numpy as jnp
from jax import lax
from jax.experimental import pallas as pl
from jax.experimental.pallas import tpu as pltpu
from jax.sharding import PartitionSpec as P

BLK = 64
CB = 16
NB = 16
TC = 128
CAP = 4
ITERS = 3
ENT = 64
SOIL = 16
BODIES = SOIL * NB
WIDE = 6 * BLK
TALL = 3 * BLK
SHARED = 32
ROWS = SOIL * SHARED
FORCE_ROWS = 3 * ENT
SEND_FIRST = FORCE_ROWS + 3 * NB + 8
SHARE_ROWS = 3 * SHARED
SEND_SECOND = SHARE_ROWS + 16
SEND_THIRD = SHARE_ROWS + 8

step_size = 0.1
hold_eps = 1e-06

bf16, f32, i32 = jnp.bfloat16, jnp.float32, jnp.int32

IN_HBM = pl.BlockSpec(memory_space=pltpu.HBM)
VECTOR = pl.BlockSpec(memory_space=pltpu.VMEM)
SCALAR = pl.BlockSpec(memory_space=pltpu.SMEM)


def momentum_weights(number):
    nesterov = 1.0
    weights = []
    for iteration in range(number):
        following = 0.5 * (-nesterov * nesterov + nesterov * math.sqrt(nesterov * nesterov + 4.0))
        weights.append(nesterov * (1.0 - nesterov) / (nesterov * nesterov + following))
        nesterov = following
    return weights


def resident(shape, dtype):
    return pltpu.VMEM(shape, dtype)


def keep(array):
    return pltpu.with_memory_space_constraint(array, pltpu.VMEM)


def far(array):
    return pltpu.with_memory_space_constraint(array, pltpu.HBM)


def shape_of(shape, dtype):
    return jax.ShapeDtypeStruct(shape, dtype)


def params(megabytes):
    return pltpu.CompilerParams(vmem_limit_bytes=megabytes << 20)


def iota(shape, dim):
    return lax.broadcasted_iota(i32, shape, dim)


def ones_where(mask):
    return jnp.where(mask, 1.0, 0.0).astype(bf16)


def dot(left, right):
    return jnp.dot(left, right, preferred_element_type=f32)


def dot_rows(left, right):
    return lax.dot_general(left, right, (((1,), (1,)), ((), ())), preferred_element_type=f32)


def planes(values):
    return [values[:, 128 * c : 128 * c + 128] for c in range(3)]


def side_by_side(rows, size):
    return jnp.concatenate([rows[size * c : size * c + size] for c in range(3)], axis=1)


def split_terms(values, terms):
    parts = []
    for _ in range(terms):
        part = values.astype(bf16)
        parts.append(part)
        values = values - part.astype(f32)
    return jnp.concatenate(parts, axis=0)


def order(block):
    return ((block & 1) << 3) + (block >> 1)


def lanes_low(shape):
    return iota(shape, len(shape) - 1) < BLK


def both(values, upper):
    low = lanes_low(values.shape)
    turned = pltpu.roll(values, BLK, 1)
    return jnp.where(low, turned, values) if upper else jnp.where(low, values, turned)


def lane_tiles(ref, row):
    return jnp.concatenate([ref[row : row + 1, 128 * t : 128 * t + 128] for t in range(8)], axis=0)


def doubled(ref, row):
    tiles = lane_tiles(ref, row)
    return jnp.concatenate([both(tiles, False), both(tiles, True)], axis=0)


def twice(normal, first, second):
    low = lanes_low((CB, 2 * BLK))
    return jnp.concatenate(
        [
            jnp.where(low, normal, first),
            jnp.where(low, second, normal),
            jnp.where(low, first, second),
        ],
        axis=1,
    ).astype(bf16)


def entry_mask():
    column = iota((16, 16 * TALL), 1)
    first = iota((16, 16 * TALL), 0) * TALL
    return ones_where((column >= first) & (column < first + TALL))


def push(picked, tiles, forces):
    mask = entry_mask()

    def group(number):
        rows = picked[pl.ds(16 * number, 16)]
        spread = jnp.concatenate([rows] * 8, axis=1) * mask
        weights = tiles[pl.ds(16 * number, 16)].reshape(16 * TALL, WIDE)
        forces[pl.ds(16 * number, 16)] = dot(spread, weights)

    def step(number, carry):
        group(number)
        group(number + 2)
        return carry

    lax.fori_loop(0, 2, step, 0)


def pull(wanted, pick_t, flipped):
    row = iota((16, WIDE), 0)
    lower, upper = [], []
    for part in range(2):
        sides = []
        for half in range(2):
            start = 32 * half + 16 * part
            rows = wanted[start : start + 16]
            sides.append(
                jnp.concatenate(
                    [rows * ones_where(row == pair) for pair in range(16)], axis=1
                )
            )
        weights = flipped[16 * part : 16 * part + 16].reshape(16 * WIDE, WIDE)
        terms = dot(jnp.concatenate(sides, axis=0), weights)
        lower.append(terms[0:16])
        upper.append(terms[16:32])
    terms = jnp.concatenate(lower + upper, axis=0)
    wrong = (iota((ENT, WIDE), 0) < ENT // 2) == (iota((ENT, WIDE), 1) >= TALL)
    sums = dot(pick_t, split_terms(jnp.where(wrong, 0.0, terms), 3))
    left, middle, right = sums[:, 0:128], sums[:, 128:256], sums[:, 256:384]
    return (
        both(left, False) + both(middle, True),
        both(left, True) + both(right, False),
        both(middle, False) + both(right, True),
    )


def tire_row(normal, first, second):
    low = lanes_low((1, 128))
    return jnp.concatenate(
        [jnp.where(low, part[0:1], part[8:9]) for part in (normal, first, second)], axis=1
    )


def eye(size):
    return ones_where(iota((size, size), 0) == iota((size, size), 1))


def first_kernel(
    count,
    owner_far,
    body_far,
    block_far,
    warm_far,
    right_far,
    rough_far,
    mass_far,
    tiles_far,
    payload,
    tiles,
    flipped,
    pick_out,
    pick_t_out,
    id_out,
    slot_out,
    slot_row,
    warm_out,
    right_out,
    rough_out,
    mass_out,
    owner,
    body,
    block,
    warm,
    right,
    rough,
    mass,
    picked,
    forces,
    sems,
    tile_sems,
):
    small = [
        pltpu.make_async_copy(source, target, sems.at[n])
        for n, (source, target) in enumerate(
            [
                (block_far, block),
                (warm_far, warm),
                (owner_far, owner),
                (body_far, body),
                (mass_far, mass),
                (right_far, right),
                (rough_far, rough),
            ]
        )
    ]
    copies = []
    for start in (0, 32, 8, 40, 16, 48, 24, 56):
        part = pl.ds(start, 8)
        copies.append(
            pltpu.make_async_copy(tiles_far.at[part], tiles.at[part], tile_sems.at[start // 8])
        )
    for copy in small + copies:
        copy.start()
    for copy in small:
        copy.wait()
    live = iota((1, ENT), 1) < count[0]
    pick_t = ones_where((iota((CB, ENT), 0) == order(block[...])) & live)
    pick = dot_rows(eye(ENT), pick_t).astype(bf16)
    pick_out[...] = pick
    pick_t_out[...] = jnp.concatenate([pick_t] * 3, axis=1)
    advance = [doubled(warm, piece) for piece in range(3)]
    picked[...] = dot(pick, twice(*advance))
    def tile_part(part):
        copies[2 * part].wait()
        copies[2 * part + 1].wait()

        for number in range(8):
            near, away = 8 * part + number, 32 + 8 * part + number
            above, below = tiles[near], tiles[away]
            flipped[near] = jnp.concatenate([above, below], axis=0).T
            for entry, tile in ((near, above), (away, below)):
                line = picked[entry : entry + 1, 0:TALL].astype(bf16)
                forces[entry : entry + 1] = dot(line, tile)

    tile_part(0)
    for piece in range(3):
        warm_out[piece] = advance[piece]
        right_out[piece] = doubled(right, piece)
    rough_out[...] = doubled(rough, 0)
    low = lanes_low((8, 128))
    lanes = []
    for piece in range(3):
        even, odd = lane_tiles(mass, 2 * piece), lane_tiles(mass, 2 * piece + 1)
        lanes.append(
            jnp.concatenate(
                [
                    jnp.where(low, even, pltpu.roll(odd, BLK, 1)),
                    jnp.where(low, pltpu.roll(even, BLK, 1), odd),
                ],
                axis=0,
            )
        )
    mass_tiles = jnp.concatenate(lanes, axis=1)
    mass_out[...] = mass_tiles
    ids = jnp.where(live, owner[...] * NB + order(body[...]), -1)
    hits_t = ones_where(iota((BODIES, ENT), 0) == ids)
    counts = dot_rows(jnp.ones((8, ENT), bf16), hits_t)
    named = jnp.where(counts > 0, 1.0, 0.0)

    owner_row = jnp.where(live, owner[...], -1)
    owner_hit = ones_where(iota((SOIL, ENT), 0) == owner_row)
    earlier = ones_where(iota((ENT, ENT), 0) < iota((ENT, ENT), 1))
    rank = jnp.sum(dot(owner_hit, earlier) * owner_hit.astype(f32), axis=0, keepdims=True)
    slot = jnp.where(live, (owner_row * 16).astype(f32) + rank, -100.0)
    slot_row[...] = jnp.broadcast_to(slot, (8, ENT))
    slot_four = jnp.where(live, (owner_row * CAP).astype(f32) + rank, -100.0)
    chosen_four = ones_where(iota((ENT, ENT), 0).astype(f32) == slot_four)
    label = jnp.where(live, order(body[...]) + 1, 0).astype(bf16)
    label_row = dot_rows(jnp.broadcast_to(label, (8, ENT)), chosen_four)
    id_row = jnp.broadcast_to((ids + 1).astype(f32), (8, ENT))
    label_row = jnp.concatenate([label_row, label_row], axis=1)
    id_row = jnp.concatenate([id_row, id_row], axis=1)
    place = iota((8, 128), 0)
    tail = jnp.zeros((8, 128), f32)
    for number, line in enumerate(
        planes(tire_row(*advance)) + [id_row, named[:, 0:128], named[:, 128:256], label_row]
    ):
        tail = jnp.where(place == number, line, tail)
    tail = tail.astype(bf16)
    mass_high = mass_tiles.astype(bf16)
    for peer in range(SOIL):
        for c, plane in enumerate(planes(mass_high)):
            payload[peer, FORCE_ROWS + NB * c : FORCE_ROWS + NB * c + NB] = plane
        payload[peer, FORCE_ROWS + 3 * NB :] = tail
    for_columns = jnp.concatenate(
        [
            jnp.broadcast_to(slot, (8, ENT)),
            jnp.broadcast_to(ids.astype(f32), (8, ENT)),
        ],
        axis=0,
    )
    columns = dot_rows(eye(ENT), for_columns.astype(bf16))
    slot_out[...] = jnp.broadcast_to(columns[:, 0:1], (ENT, 128))
    id_out[...] = jnp.broadcast_to(columns[:, 8:9], (ENT, 128))

    for part in range(1, 4):
        tile_part(part)
    sent = planes(forces[...].astype(bf16))
    for peer in range(SOIL):
        for c in range(3):
            payload[peer, ENT * c : ENT * c + ENT] = sent[c]


def slot_hits(me, slot_labels):
    column = iota((128, 128), 1)
    row = iota((128, 128), 0)
    mine = ones_where((row == me * CAP + (column >> 4)) & (column < CAP * NB))
    labels = dot(slot_labels.astype(bf16), mine)
    hits = ones_where(labels == ((iota((SOIL, 128), 1) & 15) + 1).astype(f32))
    peer = ones_where((iota((16 * SOIL, SOIL), 0) >> 4) == iota((16 * SOIL, SOIL), 1))
    return dot(peer, hits)


def mass_slots(rows):
    place = iota((16 * SOIL, 128), 0) & 15
    slot = iota((16 * SOIL, 128), 1) >> 4
    low = lanes_low((16 * SOIL, 128))
    shifted = slot - jnp.where(low, 0, CAP)
    first = jnp.where(shifted + jnp.where(low, 3, 3 + CAP) == place, both(rows, False), 0.0)
    second = jnp.where((slot + 3 + 2 * CAP == place) & low, rows, 0.0)
    return jnp.concatenate([first, second], axis=1).astype(bf16)


def owner_slots(rows, gather):
    place = iota((16 * SOIL, 128), 0) & 15
    slot = iota((16 * SOIL, 128), 1) >> 4
    fold = ones_where((iota((NB, 128), 1) & 15) == iota((NB, 128), 0))
    for c in range(3):
        chosen = jnp.where((slot + CAP * c == place) & (slot < CAP), rows, 0.0).astype(bf16)
        gather[NB * c : NB * c + NB] = dot_rows(fold, chosen).astype(bf16)


def match_shares(me, all_named, id_column, share, share_t, own):
    mine = iota((SOIL, BODIES), 0) == me
    named = jnp.sum(jnp.where(mine, all_named, 0.0), axis=0, keepdims=True)
    hits = ones_where(id_column == iota((ENT, BODIES), 1).astype(f32))
    hits_two = jnp.concatenate([hits, hits], axis=0)
    common = jnp.where(mine, 0.0, all_named * named)
    earlier = ones_where(iota((BODIES, BODIES), 0) < iota((BODIES, BODIES), 1))
    slots = jnp.where(common > 0, dot(common.astype(bf16), earlier) + 1.0, 0.0).astype(bf16)
    rank_t = dot_rows(hits, slots).astype(bf16)
    lane_start = iota((SOIL, ROWS), 0) * SHARED
    lanes = iota((SOIL, ROWS), 1)
    spread_lanes = ones_where((lanes >= lane_start) & (lanes < lane_start + SHARED))
    lane_rank = ((iota((ENT, ROWS), 1) & (SHARED - 1)) + 1).astype(f32)
    share_t[...] = ones_where(dot(rank_t, spread_lanes) == lane_rank)
    rank_two = dot_rows(slots, hits_two).astype(bf16)
    row_start = iota((ROWS, SOIL), 1) * SHARED
    row = iota((ROWS, SOIL), 0)
    spread_rows = ones_where((row >= row_start) & (row < row_start + SHARED))
    row_rank = ((iota((ROWS, 128), 0) & (SHARED - 1)) + 1).astype(f32)
    share[...] = ones_where(dot(spread_rows, rank_two) == row_rank)
    own[...] = dot_rows(hits, hits_two).astype(bf16)


def project_cone(normal, tangent_one, tangent_two, friction):
    tangent_size = jnp.sqrt(tangent_one * tangent_one + tangent_two * tangent_two)
    inside = tangent_size <= friction * normal
    polar_side = friction * tangent_size <= -normal
    middle = jnp.logical_not(jnp.logical_or(inside, polar_side))
    safe_size = jnp.where(middle, tangent_size, 1.0)
    new_normal = (friction * tangent_size + normal) / (1.0 + friction * friction)
    shrink = friction * new_normal / safe_size
    out_normal = jnp.where(inside, normal, jnp.where(polar_side, 0.0, new_normal))
    factor = jnp.where(inside, 1.0, jnp.where(polar_side, 0.0, shrink))
    return out_normal, tangent_one * factor, tangent_two * factor


def step_kernel(
    weight,
    is_first,
    is_last,
    arrived,
    pick,
    pick_t,
    tiles,
    flipped,
    current,
    advance,
    right_side,
    friction,
    *rest,
):
    copy = None
    if is_first:
        id_column, mass_in, matrix_far = rest[0:3]
        payload, new_current, new_advance, new_forces, mass_rows = rest[3:8]
        share, share_t, own, matrix, slot_labels = rest[8:13]
        spread, picked, sem = rest[13:]
        copy = pltpu.make_async_copy(matrix_far, matrix, sem)
        copy.start()
        me = lax.axis_index("soil")
        mine = id_column[:, 0:1]
        tail = arrived[:, FORCE_ROWS + 3 * NB :, :].astype(f32)
        tail = tail.reshape(8 * SOIL, 128).astype(bf16)
        tail_lane = iota((7 * SOIL, 8 * SOIL), 1)
        tail_row = iota((7 * SOIL, 8 * SOIL), 0)
        tails = dot(
            ones_where(tail_lane == (tail_row & (SOIL - 1)) * 8 + (tail_row >> 4)), tail
        )
        tire_all = side_by_side(tails, SOIL)
        names = tails[3 * SOIL : 4 * SOIL]
        all_named = jnp.concatenate(
            [tails[4 * SOIL : 5 * SOIL], tails[5 * SOIL : 6 * SOIL]], axis=1
        )
        low_lanes = lanes_low((1, 128))
        own_name = jnp.where(mine >= 0, mine + 1.0, -1.0)
        match = jnp.concatenate(
            [
                ones_where(
                    own_name
                    == jnp.where(
                        low_lanes, names[2 * t : 2 * t + 1], names[2 * t + 1 : 2 * t + 2]
                    )
                )
                for t in range(SOIL // 2)
            ],
            axis=1,
        )
        name_pick = ones_where(mine == iota((ENT, BODIES), 1).astype(f32))
        found, sums = [], []
        for c in range(3):
            start = FORCE_ROWS + NB * c
            found.append(dot(name_pick, arrived[:, start : start + NB, :].reshape(BODIES, 128)))
            plane = arrived[:, ENT * c : ENT * c + ENT, :].reshape(SOIL * ENT, 128)
            sums.append(dot(match, plane))
        mass_high = jnp.concatenate(found, axis=1)
        mass_rows[...] = mass_high
        wanted = jnp.concatenate(sums, axis=1) * mass_high
        match_shares(me, all_named, mine, share, share_t, own)
        slot_labels[...] = tails[6 * SOIL : 7 * SOIL]
        tail_pick = mass_slots(slot_hits(me, tails[6 * SOIL : 7 * SOIL]))
        mass_low = (mass_in[...] - mass_in[...].astype(bf16).astype(f32)).astype(bf16)
        tail_rows = dot(
            tail_pick,
            jnp.concatenate(
                [plane for plane in planes(mass_low) for _ in range(CAP)]
                + [jnp.zeros((CAP * NB, 128), bf16)],
                axis=0,
            ),
        )
    else:
        forces_in, mass_in, share, share_t, own, matrix = rest[0:6]
        if is_last:
            outputs, (spread, picked) = rest[6:-2], rest[-2:]
        else:
            slot_column, outputs, (spread, picked) = rest[6], rest[7:-2], rest[-2:]
        size = 8 if is_last else 16
        tail = arrived[:, SHARE_ROWS:, :].astype(f32).reshape(size * SOIL, 128).astype(bf16)
        tail_lane = iota((3 * SOIL, size * SOIL), 1)
        tail_row = iota((3 * SOIL, size * SOIL), 0)
        tire_all = side_by_side(
            dot(
                ones_where(tail_lane == (tail_row & (SOIL - 1)) * size + (tail_row >> 4)), tail
            ),
            SOIL,
        )
        received = [
            arrived[:, SHARED * c : SHARED * c + SHARED, :].reshape(ROWS, 128) for c in range(3)
        ]
        sums = jnp.concatenate([dot(share_t[...], plane) for plane in received], axis=1)
        sums += dot(own[...], split_terms(forces_in[...], 2))
        mass_all = mass_in[...]
        if not is_last:
            lane = iota((ENT, 16 * SOIL), 1).astype(f32)
            first = slot_column[:, 0:1] + 3.0
            chosen = [ones_where(lane == first + float(CAP * c)) for c in range(3)]
            mass_all += side_by_side(dot(jnp.concatenate(chosen, axis=0), tail), ENT)
        wanted = sums * mass_all
    pieces = pull(wanted.astype(bf16), pick_t[...], flipped)

    device = iota((SOIL, WIDE), 0)
    for peer in range(SOIL):
        spread[:, WIDE * peer : WIDE * peer + WIDE] = jnp.where(
            device == peer, tire_all, 0.0
        ).astype(bf16)
    if copy is not None:
        copy.wait()
    tire = jnp.sum(dot(spread[...], matrix[...]), axis=0, keepdims=True)

    row = iota((CB, 128), 0)
    moved = []
    for piece in range(3):
        line = jnp.broadcast_to(tire[:, 128 * piece : 128 * piece + 128], (CB, 128))
        added = jnp.where(
            row == 0, both(line, False), jnp.where(row == 8, both(line, True), 0.0)
        )
        gradient = pieces[piece] + added + right_side[piece]
        moved.append(advance[piece] - step_size * gradient)
    updated = project_cone(*moved, friction[...])
    change = [updated[piece] - current[piece] for piece in range(3)]
    if is_last:
        impulses, doubles, squares = outputs
        low = lanes_low((8, 128))
        for piece in range(3):
            merged = jnp.where(low, updated[piece][0:8], updated[piece][8:16])
            for t in range(8):
                impulses[piece : piece + 1, 128 * t : 128 * t + 128] = merged[t : t + 1]
        doubles[...] = twice(*updated)
        total = change[0] * change[0] + change[1] * change[1] + change[2] * change[2]
        total = jnp.where(lanes_low((CB, 128)), total, 0.0)
        total = jnp.sum(jnp.sum(total, axis=1, keepdims=True), axis=0, keepdims=True)
        squares[...] = jnp.broadcast_to(total.reshape(1, 1, 1), squares.shape)
        return
    if not is_first:
        payload, new_current, new_advance, new_forces, mass_rows = outputs
        mass_rows[...] = mass_all
    ahead = [updated[piece] + weight * change[piece] for piece in range(3)]
    for piece in range(3):
        new_current[piece] = updated[piece]
        new_advance[piece] = ahead[piece]
    picked[...] = dot(pick[...], twice(*ahead)).astype(bf16)
    push(picked, tiles, new_forces)
    shares = dot(share[...], split_terms(new_forces[...], 2)).astype(bf16)
    for c, plane in enumerate(planes(shares)):
        payload[:, SHARED * c : SHARED * c + SHARED, :] = plane.reshape(SOIL, SHARED, 128)
    size = 16 if is_first else 8
    place = iota((size * SOIL, 128), 0) & (size - 1)
    tail_out = tail_rows if is_first else jnp.zeros((size * SOIL, 128), f32)
    for c, line in enumerate(planes(tire_row(*ahead))):
        tail_out = jnp.where(place == c, line, tail_out)
    payload[:, SHARE_ROWS:, :] = tail_out.reshape(SOIL, size, 128).astype(bf16)


def last_push_kernel(
    doubles, pick, slot_row, slot_labels, tiles_far, forces, owner_pick, gather, tiles, sems
):
    copies = [
        pltpu.make_async_copy(
            tiles_far.at[pl.ds(16 * g, 16)], tiles.at[pl.ds(16 * g, 16)], sems.at[g]
        )
        for g in range(4)
    ]
    for copy in copies:
        copy.start()
    picked = dot(pick[...], doubles[...]).astype(bf16)
    mask = entry_mask()
    for group in range(4):
        copies[group].wait()
        part = slice(16 * group, 16 * group + 16)
        spread = jnp.concatenate([picked[part]] * 8, axis=1) * mask
        forces[part] = dot(spread, tiles[part].reshape(16 * TALL, WIDE))
        if group == 0:
            line = iota((16 * SOIL, ENT), 0).astype(f32)
            chosen = [ones_where(line == slot_row[0:1] + float(CAP * c)) for c in range(3)]
            owner_pick[...] = jnp.concatenate([part for part in chosen for _ in range(3)], axis=1)
        if group == 1:
            owner_slots(slot_hits(lax.axis_index("soil"), slot_labels[...]), gather)


def outgoing_kernel(forces, owner_pick, across, payload):
    terms = [split_terms(plane, 3) for plane in planes(forces[...])]
    rows = dot(owner_pick[...], jnp.concatenate(terms, axis=0))
    squares = jnp.sum(across[:, 0, :], axis=0, keepdims=True)[:, 0:1]
    place = iota((16 * SOIL, 128), 0) & 15
    payload[...] = jnp.where(place == 3 * CAP, squares, rows).reshape(SOIL, 16, 128)


def totals_kernel(scale, arrived, gather, mass, velocity, norm):
    rows = arrived[...].reshape(16 * SOIL, 128)
    is_square = (iota((16 * SOIL, 128), 0) & 15) == 3 * CAP
    squares = jnp.sum(jnp.where(is_square, rows, 0.0), axis=0, keepdims=True)
    norm[...] = jnp.sqrt(squares[:, 0:1] * scale + hold_eps) / step_size
    totals = dot(jnp.concatenate([gather[...]] * 3, axis=1), split_terms(rows, 3))
    totals = side_by_side(totals, NB) * mass[...]
    low = lanes_low((8, 128))
    for piece in range(3):
        tile = totals[:, 128 * piece : 128 * piece + 128]
        even, odd = tile[0:8], tile[8:16]
        for half, merged in enumerate(
            (
                jnp.where(low, even, pltpu.roll(odd, BLK, 1)),
                jnp.where(low, pltpu.roll(even, BLK, 1), odd),
            )
        ):
            component = 2 * piece + half
            for t in range(8):
                velocity[component : component + 1, 128 * t : 128 * t + 128] = merged[t : t + 1]


def step_scratch():
    return [pltpu.VMEM((SOIL, SOIL * 3 * TC), bf16), pltpu.VMEM((ENT, WIDE), bf16)]


def on_device(
    warm_start,
    right_side,
    friction,
    inverse_mass,
    jacobian,
    compliance,
    entry_block,
    entry_owner,
    entry_body,
    block_count,
):
    regions = lax.axis_size("grp")
    contacts = warm_start.shape[1]
    elements = 3 * contacts * SOIL * regions
    state = shape_of((3, CB, 128), f32)

    def line(array):
        return far(array.reshape(1, -1))

    (
        payload,
        tiles,
        flipped,
        pick,
        pick_t,
        id_column,
        slot_column,
        slot_row,
        warm,
        right,
        rough,
        mass_tiles,
    ) = pl.pallas_call(
        first_kernel,
        out_shape=(
            shape_of((SOIL, SEND_FIRST, 128), bf16),
            resident((ENT, TALL, WIDE), bf16),
            resident((ENT // 2, WIDE, 2 * TALL), bf16),
            shape_of((ENT, CB), bf16),
            shape_of((CB, 3 * ENT), bf16),
            shape_of((ENT, 128), f32),
            shape_of((ENT, 128), f32),
            shape_of((8, ENT), f32),
            state,
            state,
            shape_of((CB, 128), f32),
            shape_of((NB, WIDE), f32),
        ),
        in_specs=[SCALAR] + [IN_HBM] * 8,
        out_specs=(VECTOR,) * 12,
        scratch_shapes=[
            pltpu.VMEM((1, ENT), i32),
            pltpu.VMEM((1, ENT), i32),
            pltpu.VMEM((1, ENT), i32),
            pltpu.VMEM((3, contacts), f32),
            pltpu.VMEM((3, contacts), f32),
            pltpu.VMEM((1, contacts), f32),
            pltpu.VMEM((6, contacts), f32),
            pltpu.VMEM((ENT, WIDE), f32),
            pltpu.VMEM((ENT, WIDE), f32),
            pltpu.SemaphoreType.DMA((7,)),
            pltpu.SemaphoreType.DMA((ENT // 8,)),
        ],
        compiler_params=params(8),
        name="first",
    )(
        block_count,
        line(entry_owner),
        line(entry_body),
        line(entry_block),
        far(warm_start),
        far(right_side),
        line(friction),
        far(inverse_mass),
        far(jacobian),
    )
    weights = momentum_weights(ITERS)
    current = warm
    advance = warm
    for iteration in range(ITERS):
        arrived = lax.all_to_all(payload, "soil", 0, 0, tiled=True)
        is_first, is_last = iteration == 0, iteration == ITERS - 1
        if is_last:
            outs = [
                shape_of((3, contacts), f32),
                shape_of((CB, WIDE), bf16),
                shape_of((regions, 1, 128), f32),
            ]
        else:
            outs = [
                shape_of((SOIL, SEND_SECOND if is_first else SEND_THIRD, 128), bf16),
                state,
                state,
                shape_of((ENT, WIDE), f32),
                shape_of((ENT, WIDE), f32),
            ]
        scratch = step_scratch()
        if is_first:
            outs += [
                shape_of((ROWS, 128), bf16),
                shape_of((ENT, ROWS), bf16),
                shape_of((ENT, 128), bf16),
                resident(compliance.shape, bf16),
                shape_of((SOIL, 128), f32),
            ]
            more = [id_column, mass_tiles, far(compliance)]
            more_specs = [VECTOR] * 2 + [IN_HBM]
            scratch.append(pltpu.SemaphoreType.DMA)
        else:
            more = [forces, mass_rows, *kept, keep(matrix)]
            if not is_last:
                more.append(slot_column)
            more_specs = [VECTOR] * len(more)
        results = pl.pallas_call(
            functools.partial(step_kernel, weights[iteration], is_first, is_last),
            out_shape=tuple(outs),
            in_specs=[VECTOR] * 9 + more_specs,
            out_specs=(VECTOR,) * len(outs),
            scratch_shapes=scratch,
            compiler_params=params(12),
            name=f"step{iteration}",
        )(
            arrived,
            pick,
            pick_t,
            keep(tiles),
            keep(flipped),
            current,
            advance,
            right,
            rough,
            *more,
        )
        if is_last:
            impulses, doubles, squares = results
            break
        payload, current, advance, forces, mass_rows = results[:5]
        if is_first:
            kept, matrix, slot_labels = results[5:8], results[8], results[9]

    across = lax.all_to_all(squares, "grp", 0, 0, tiled=True)
    forces, owner_pick, gather = pl.pallas_call(
        last_push_kernel,
        out_shape=(
            shape_of((ENT, WIDE), f32),
            shape_of((16 * SOIL, 9 * ENT), bf16),
            shape_of((3 * NB, 16 * SOIL), bf16),
        ),
        in_specs=[VECTOR] * 4 + [IN_HBM],
        out_specs=(VECTOR,) * 3,
        scratch_shapes=[
            pltpu.VMEM((ENT, TALL, WIDE), bf16),
            pltpu.SemaphoreType.DMA((4,)),
        ],
        compiler_params=params(14),
        cost_estimate=pl.CostEstimate(
            flops=10000000, bytes_accessed=10000000, transcendentals=0
        ),
        name="last_push",
    )(doubles, pick, slot_row, slot_labels, far(jacobian))
    outgoing = pl.pallas_call(
        outgoing_kernel,
        out_shape=shape_of((SOIL, 16, 128), f32),
        in_specs=[VECTOR] * 3,
        out_specs=VECTOR,
        compiler_params=params(6),
        name="outgoing",
    )(forces, owner_pick, across)
    arrived = lax.all_to_all(outgoing, "soil", 0, 0, tiled=True)
    velocity, norm = pl.pallas_call(
        functools.partial(totals_kernel, 1.0 / elements),
        out_shape=(shape_of((6, contacts), f32), shape_of((1, 1), f32)),
        in_specs=[VECTOR] * 3,
        out_specs=(VECTOR, VECTOR),
        compiler_params=params(4),
        name="totals",
    )(arrived, gather, mass_tiles)
    return (impulses, velocity, norm[0, 0])


def solution(mesh):
    placed = (
        P(None, ("grp", "soil")),
        P(None, ("grp", "soil")),
        P(("grp", "soil")),
        P(None, ("grp", "soil")),
        P(("grp", "soil"), None, None),
        P(None, "soil"),
        P(("grp", "soil")),
        P(("grp", "soil")),
        P(("grp", "soil")),
        P(("grp", "soil")),
    )
    return jax.shard_map(
        on_device,
        mesh=mesh,
        in_specs=placed,
        out_specs=(P(None, ("grp", "soil")), P(None, ("grp", "soil")), P()),
        check_vma=False,
    )
```

profile of v0, /device:TPU:0, one launch (start us, length us, event | category | flops | bytes accessed | tf_op | source)
XLA Modules:
  0.0 92.3 jit_solution(15778626701848974218)
XLA Ops:
  1.3 6.4 %first.1 = (bf16[16,248,128]{2,1,0:T(8,128)(2,1)S(1)}, bf16[64,192,384]{2,1,0:T(8,128)(2,1)S(1)}, bf16[32,384,384]{2,1,0:T(8,128)(2,1)S(1)}, bf16[64,16]{1,0:T(8...) custom-call(s32[1]{0:T(128)S(6)} %copy.13.count, ...), custom_call_target="tpu_custom_call" | custom-call | tf_op jit(solution)/shard_map/first/pallas_call | solution.py:660
  7.7 24.7 %all_to_all.25.arrived = bf16[16,248,128]{2,1,0:T(8,128)(2,1)S(1)} all-to-all(bf16[16,248,128]{2,1,0:T(8,128)(2,1)S(1)} %get-tuple-element.38), channel_id=1, replica_groups=mesh['grp'=8,'soil'=16] {'soil'}, dimensions={0} | all-to-all | bytes 2031616 | tf_op jit(solution)/shard_map/all_to_all | solution.py:708
  32.4 5.5 %step0.1 = (bf16[16,112,128]{2,1,0:T(8,128)(2,1)S(1)}, f32[3,16,128]{2,1,0:T(8,128)S(1)}, f32[3,16,128]{2,1,0:T(8,128)S(1)}, f32[64,384]{1,0:T(8,128)S(1)}, f32[...) custom-call(bf16[16,248,128]{2,1,0:T(8,128)(2,1)S(1)} %all_to_all.25, ...), custom_call_target="tpu_custom_call" | custom-call | tf_op jit(solution)/shard_map/step0/pallas_call | solution.py:741
  38.0 13.0 %all_to_all.26.arrived = bf16[16,112,128]{2,1,0:T(8,128)(2,1)S(1)} all-to-all(bf16[16,112,128]{2,1,0:T(8,128)(2,1)S(1)} %get-tuple-element.48), channel_id=1, replica_groups=mesh['grp'=8,'soil'=16] {'soil'}, dimensions={0} | all-to-all | bytes 917504 | tf_op jit(solution)/shard_map/all_to_all | solution.py:708
  50.9 4.3 %step1.1 = (bf16[16,104,128]{2,1,0:T(8,128)(2,1)S(1)}, f32[3,16,128]{2,1,0:T(8,128)S(1)}, f32[3,16,128]{2,1,0:T(8,128)S(1)}, f32[64,384]{1,0:T(8,128)S(1)}, f32[64,384]{1,0:T(8,128)S(1)}) custom-call(bf16[16,112,128]{2,1,0:T(8,128)(2,1)S(1)} %all_to_all.26.arrived, bf16[64,16]{1,0:T(8,128)(2,1)S(1)} %get-tuple-element.39.pick, ...), custom_call_target="tpu_custom_call" | custom-call | tf_op jit(solution)/shard_map/step1/pallas_call | solution.py:741
  55.3 12.5 %all_to_all.27.arrived = bf16[16,104,128]{2,1,0:T(8,128)(2,1)S(1)} all-to-all(bf16[16,104,128]{2,1,0:T(8,128)(2,1)S(1)} %get-tuple-element.58), channel_id=1, replica_groups=mesh['grp'=8,'soil'=16] {'soil'}, dimensions={0} | all-to-all | bytes 851968 | tf_op jit(solution)/shard_map/all_to_all | solution.py:708
  67.7 3.1 %step2.1 = (f32[3,1024]{1,0:T(4,128)}, bf16[16,384]{1,0:T(8,128)(2,1)S(1)}, f32[8,1,128]{2,1,0:T(1,128)}) custom-call(bf16[16,104,128]{2,1,0:T(8,128)(2,1)S(1)} %all_to_all.27.arrived, bf16[64,16]{1,0:T(8,128)(2,1)S(1)} %get-tuple-element.39.pick, bf16[16,192]{1,0:T(8,128)(2,1)S(1)} %get-tuple-element.40.pick_t, ...), custom_call_target="tpu_custom_call" | custom-call | tf_op jit(solution)/shard_map/step2/pallas_call | solution.py:741
  70.8 4.3 %all-to-all-start.3 = ((f32[8,1,128]{2,1,0:T(1,128)}), f32[8,1,128]{2,1,0:T(1,128)S(1)}, u32[]{:S(2)}, u32[]{:S(2)}) async-start(f32[8,1,128]{2,1,0:T(1,128)} %get-tuple-element.69), calls=%async_computation.3 | async-start | bytes 8192 | tf_op jit(solution)/shard_map/all_to_all | solution.py:768
  75.1 4.3 %last_push.1 = (f32[64,384]{1,0:T(8,128)S(1)}, bf16[256,576]{1,0:T(8,128)(2,1)S(1)}, bf16[48,256]{1,0:T(8,128)(2,1)S(1)}) custom-call(bf16[16,384]{1,0:T(8,128)(2,1)S(1)} %get-tuple-element.64.doubles, bf16[64,16]{1,0:T(8,128)(2,1)S(1)} %get-tuple-element.39.pick, f32[8,64]{1,0:T(8,128)S(1)} %get-tuple-element.65.slot_row, ...), custom_call_target="tpu_custom_call" | custom-call | flops 10000000 | bytes 10000000 | tf_op jit(solution)/shard_map/last_push/pallas_call | solution.py:769
  79.4 0.9 all-to-all-done.3.across
  80.3 0.2 outgoing.1
  80.6 10.9 %all_to_all.28.arrived = f32[16,16,128]{2,1,0:T(8,128)S(1)} all-to-all(f32[16,16,128]{2,1,0:T(8,128)S(1)} %outgoing.1), channel_id=1, replica_groups=mesh['grp'=8,'soil'=16] {'soil'}, dimensions={0} | all-to-all | bytes 262144 | tf_op jit(solution)/shard_map/all_to_all | solution.py:796
  91.5 0.9 totals.1
Async XLA Ops:
  70.8 9.5 %all-to-all-start.3 = ((f32[8,1,128]{2,1,0:T(1,128)}), f32[8,1,128]{2,1,0:T(1,128)S(1)}, u32[]{:S(2)}, u32[]{:S(2)}) async-start(f32[8,1,128]{2,1,0:T(1,128)} %get-tuple-element.69), calls=%async_computation.3 | async-start | bytes 8192 | tf_op jit(solution)/shard_map/all_to_all | solution.py:768
where the time goes:
time: 92.6 us; the launch traced here: 92.3 us
  blocking collectives  61.1 us (66%)
  Pallas kernels  24.8 us (27%)
  starting transfers between devices  4.31 us (5%)
  between operations  1.32 us (1%)
    all_to_all x3, blocking collectives, on_device(): arrived = lax.all_to_all(payload, 'soil', 0, 0, tiled=True)  50.2 us
    pallas_call x3, Pallas kernels, on_device(): pl.pallas_call(functools.partial(step_kernel, weights[iteration], is_firs...  12.9 us
    all_to_all x1, blocking collectives, on_device(): arrived = lax.all_to_all(outgoing, 'soil', 0, 0, tiled=True)  10.9 us
    pallas_call x1, Pallas kernels, on_device(): pl.pallas_call(first_kernel, out_shape=(shape_of((SOIL, SEND_FIRST, 128),...  6.41 us
    pallas_call x1, Pallas kernels, on_device(): pl.pallas_call(last_push_kernel, out_shape=(shape_of((ENT, WIDE), f32), s...  4.32 us
    all_to_all x1, starting transfers between devices, on_device(): across = lax.all_to_all(squares, 'grp', 0, 0, tiled=True)  4.31 us
  transfers between devices with their start and end apart: 1, of which 1 were waited for; matrix products, arithmetic and copies ran while one was open for 0% of the time, Pallas kernels for 5%

commit v1 on v0

--- a/solution.py
+++ b/solution.py
@@ -251,9 +251,9 @@
         copies.append(
             pltpu.make_async_copy(tiles_far.at[part], tiles.at[part], tile_sems.at[start // 8])
         )
-    for copy in small + copies:
+    for copy in small + copies[0 : 2 * 2]:
         copy.start()
-    for copy in small:
+    for copy in small[0:2]:
         copy.wait()
     live = iota((1, ENT), 1) < count[0]
     pick_t = ones_where((iota((CB, ENT), 0) == order(block[...])) & live)
@@ -262,10 +262,12 @@
     pick_t_out[...] = jnp.concatenate([pick_t] * 3, axis=1)
     advance = [doubled(warm, piece) for piece in range(3)]
     picked[...] = dot(pick, twice(*advance))
+
     def tile_part(part):
         copies[2 * part].wait()
         copies[2 * part + 1].wait()
-
+        for copy in copies[2 * (part + 2) : 2 * (part + 2) + 2]:
+            copy.start()
         for number in range(8):
             near, away = 8 * part + number, 32 + 8 * part + number
             above, below = tiles[near], tiles[away]
@@ -274,6 +276,8 @@
                 line = picked[entry : entry + 1, 0:TALL].astype(bf16)
                 forces[entry : entry + 1] = dot(line, tile)
 
+    for copy in small[2:]:
+        copy.wait()
     tile_part(0)
     for piece in range(3):
         warm_out[piece] = advance[piece]
@@ -303,6 +307,7 @@
     owner_hit = ones_where(iota((SOIL, ENT), 0) == owner_row)
     earlier = ones_where(iota((ENT, ENT), 0) < iota((ENT, ENT), 1))
     rank = jnp.sum(dot(owner_hit, earlier) * owner_hit.astype(f32), axis=0, keepdims=True)
+    tile_part(1)
     slot = jnp.where(live, (owner_row * 16).astype(f32) + rank, -100.0)
     slot_row[...] = jnp.broadcast_to(slot, (8, ENT))
     slot_four = jnp.where(live, (owner_row * CAP).astype(f32) + rank, -100.0)
@@ -312,6 +317,7 @@
     id_row = jnp.broadcast_to((ids + 1).astype(f32), (8, ENT))
     label_row = jnp.concatenate([label_row, label_row], axis=1)
     id_row = jnp.concatenate([id_row, id_row], axis=1)
+    tile_part(2)
     place = iota((8, 128), 0)
     tail = jnp.zeros((8, 128), f32)
     for number, line in enumerate(
@@ -335,8 +341,7 @@
     slot_out[...] = jnp.broadcast_to(columns[:, 0:1], (ENT, 128))
     id_out[...] = jnp.broadcast_to(columns[:, 8:9], (ENT, 128))
 
-    for part in range(1, 4):
-        tile_part(part)
+    tile_part(3)
     sent = planes(forces[...].astype(bf16))
     for peer in range(SOIL):
         for c in range(3):
@@ -386,12 +391,11 @@
     spread_lanes = ones_where((lanes >= lane_start) & (lanes < lane_start + SHARED))
     lane_rank = ((iota((ENT, ROWS), 1) & (SHARED - 1)) + 1).astype(f32)
     share_t[...] = ones_where(dot(rank_t, spread_lanes) == lane_rank)
-    rank_two = dot_rows(slots, hits_two).astype(bf16)
-    row_start = iota((ROWS, SOIL), 1) * SHARED
-    row = iota((ROWS, SOIL), 0)
-    spread_rows = ones_where((row >= row_start) & (row < row_start + SHARED))
-    row_rank = ((iota((ROWS, 128), 0) & (SHARED - 1)) + 1).astype(f32)
-    share[...] = ones_where(dot(spread_rows, rank_two) == row_rank)
+    rank_two = dot_rows(slots, hits_two)
+    order_row = (iota((SHARED, 128), 0) + 1).astype(f32)
+    for peer in range(SOIL):
+        line = jnp.broadcast_to(rank_two[peer : peer + 1], (SHARED, 128))
+        share[SHARED * peer : SHARED * peer + SHARED] = ones_where(line == order_row)
     own[...] = dot_rows(hits, hits_two).astype(bf16)
 
 

time: 92.6 us -> 91.4 us (0.987)
  Pallas kernels: 24.8 us -> 23.5 us
    pallas_call x1, Pallas kernels: 6.41 us -> 5.13 us  [on_device(): pl.pallas_call(first_kernel, out_shape=(shape_of((SOIL, SEND_FIRST, 128),...]
where the time goes in v1:
time: 91.4 us; the launch traced here: 91 us
  blocking collectives  61.1 us (67%)
  Pallas kernels  23.5 us (26%)
  starting transfers between devices  4.3 us (5%)
  between operations  1.32 us (1%)
    all_to_all x3, blocking collectives, on_device(): arrived = lax.all_to_all(payload, 'soil', 0, 0, tiled=True)  50.2 us
    pallas_call x3, Pallas kernels, on_device(): pl.pallas_call(functools.partial(step_kernel, weights[iteration], is_firs...  12.9 us
    all_to_all x1, blocking collectives, on_device(): arrived = lax.all_to_all(outgoing, 'soil', 0, 0, tiled=True)  10.9 us
    pallas_call x1, Pallas kernels, on_device(): pl.pallas_call(first_kernel, out_shape=(shape_of((SOIL, SEND_FIRST, 128),...  5.13 us
    pallas_call x1, Pallas kernels, on_device(): pl.pallas_call(last_push_kernel, out_shape=(shape_of((ENT, WIDE), f32), s...  4.32 us
    all_to_all x1, starting transfers between devices, on_device(): across = lax.all_to_all(squares, 'grp', 0, 0, tiled=True)  4.3 us
  transfers between devices with their start and end apart: 1, of which 1 were waited for; matrix products, arithmetic and copies ran while one was open for 0% of the time, Pallas kernels for 5%

profile of v1, /device:TPU:0, one launch (start us, length us, event | category | flops | bytes accessed | tf_op | source)
XLA Modules:
  0.0 91.0 jit_solution(4129919186485275524)
XLA Ops:
  1.3 5.1 %first.1 = (bf16[16,248,128]{2,1,0:T(8,128)(2,1)S(1)}, bf16[64,192,384]{2,1,0:T(8,128)(2,1)S(1)}, bf16[32,384,384]{2,1,0:T(8,128)(2,1)S(1)}, bf16[64,16]{1,0:T(8...) custom-call(s32[1]{0:T(128)S(6)} %copy.13.count, ...), custom_call_target="tpu_custom_call" | custom-call | tf_op jit(solution)/shard_map/first/pallas_call | solution.py:664
  6.4 24.7 %all_to_all.25.arrived = bf16[16,248,128]{2,1,0:T(8,128)(2,1)S(1)} all-to-all(bf16[16,248,128]{2,1,0:T(8,128)(2,1)S(1)} %get-tuple-element.38), channel_id=1, replica_groups=mesh['grp'=8,'soil'=16] {'soil'}, dimensions={0} | all-to-all | bytes 2031616 | tf_op jit(solution)/shard_map/all_to_all | solution.py:712
  31.2 5.5 %step0.1 = (bf16[16,112,128]{2,1,0:T(8,128)(2,1)S(1)}, f32[3,16,128]{2,1,0:T(8,128)S(1)}, f32[3,16,128]{2,1,0:T(8,128)S(1)}, f32[64,384]{1,0:T(8,128)S(1)}, f32[...) custom-call(bf16[16,248,128]{2,1,0:T(8,128)(2,1)S(1)} %all_to_all.25, ...), custom_call_target="tpu_custom_call" | custom-call | tf_op jit(solution)/shard_map/step0/pallas_call | solution.py:745
  36.7 13.0 %all_to_all.26.arrived = bf16[16,112,128]{2,1,0:T(8,128)(2,1)S(1)} all-to-all(bf16[16,112,128]{2,1,0:T(8,128)(2,1)S(1)} %get-tuple-element.48), channel_id=1, replica_groups=mesh['grp'=8,'soil'=16] {'soil'}, dimensions={0} | all-to-all | bytes 917504 | tf_op jit(solution)/shard_map/all_to_all | solution.py:712
  49.7 4.3 %step1.1 = (bf16[16,104,128]{2,1,0:T(8,128)(2,1)S(1)}, f32[3,16,128]{2,1,0:T(8,128)S(1)}, f32[3,16,128]{2,1,0:T(8,128)S(1)}, f32[64,384]{1,0:T(8,128)S(1)}, f32[64,384]{1,0:T(8,128)S(1)}) custom-call(bf16[16,112,128]{2,1,0:T(8,128)(2,1)S(1)} %all_to_all.26.arrived, bf16[64,16]{1,0:T(8,128)(2,1)S(1)} %get-tuple-element.39.pick, ...), custom_call_target="tpu_custom_call" | custom-call | tf_op jit(solution)/shard_map/step1/pallas_call | solution.py:745
  54.0 12.5 %all_to_all.27.arrived = bf16[16,104,128]{2,1,0:T(8,128)(2,1)S(1)} all-to-all(bf16[16,104,128]{2,1,0:T(8,128)(2,1)S(1)} %get-tuple-element.58), channel_id=1, replica_groups=mesh['grp'=8,'soil'=16] {'soil'}, dimensions={0} | all-to-all | bytes 851968 | tf_op jit(solution)/shard_map/all_to_all | solution.py:712
  66.5 3.1 %step2.1 = (f32[3,1024]{1,0:T(4,128)}, bf16[16,384]{1,0:T(8,128)(2,1)S(1)}, f32[8,1,128]{2,1,0:T(1,128)}) custom-call(bf16[16,104,128]{2,1,0:T(8,128)(2,1)S(1)} %all_to_all.27.arrived, bf16[64,16]{1,0:T(8,128)(2,1)S(1)} %get-tuple-element.39.pick, bf16[16,192]{1,0:T(8,128)(2,1)S(1)} %get-tuple-element.40.pick_t, ...), custom_call_target="tpu_custom_call" | custom-call | tf_op jit(solution)/shard_map/step2/pallas_call | solution.py:745
  69.5 4.3 %all-to-all-start.3 = ((f32[8,1,128]{2,1,0:T(1,128)}), f32[8,1,128]{2,1,0:T(1,128)S(1)}, u32[]{:S(2)}, u32[]{:S(2)}) async-start(f32[8,1,128]{2,1,0:T(1,128)} %get-tuple-element.69), calls=%async_computation.3 | async-start | bytes 8192 | tf_op jit(solution)/shard_map/all_to_all | solution.py:772
  73.8 4.3 %last_push.1 = (f32[64,384]{1,0:T(8,128)S(1)}, bf16[256,576]{1,0:T(8,128)(2,1)S(1)}, bf16[48,256]{1,0:T(8,128)(2,1)S(1)}) custom-call(bf16[16,384]{1,0:T(8,128)(2,1)S(1)} %get-tuple-element.64.doubles, bf16[64,16]{1,0:T(8,128)(2,1)S(1)} %get-tuple-element.39.pick, f32[8,64]{1,0:T(8,128)S(1)} %get-tuple-element.65.slot_row, ...), custom_call_target="tpu_custom_call" | custom-call | flops 10000000 | bytes 10000000 | tf_op jit(solution)/shard_map/last_push/pallas_call | solution.py:773
  78.1 0.9 all-to-all-done.3.across
  79.0 0.2 outgoing.1
  79.3 10.9 %all_to_all.28.arrived = f32[16,16,128]{2,1,0:T(8,128)S(1)} all-to-all(f32[16,16,128]{2,1,0:T(8,128)S(1)} %outgoing.1), channel_id=1, replica_groups=mesh['grp'=8,'soil'=16] {'soil'}, dimensions={0} | all-to-all | bytes 262144 | tf_op jit(solution)/shard_map/all_to_all | solution.py:800
  90.2 0.9 totals.1
Async XLA Ops:
  69.5 9.5 %all-to-all-start.3 = ((f32[8,1,128]{2,1,0:T(1,128)}), f32[8,1,128]{2,1,0:T(1,128)S(1)}, u32[]{:S(2)}, u32[]{:S(2)}) async-start(f32[8,1,128]{2,1,0:T(1,128)} %get-tuple-element.69), calls=%async_computation.3 | async-start | bytes 8192 | tf_op jit(solution)/shard_map/all_to_all | solution.py:772

commit v2 on v1

--- a/solution.py
+++ b/solution.py
@@ -159,22 +159,22 @@
 
 
 def pull(wanted, pick_t, flipped):
-    row = iota((16, WIDE), 0)
+    row = iota((8, WIDE), 0)
     lower, upper = [], []
-    for part in range(2):
+    for part in range(4):
         sides = []
         for half in range(2):
-            start = 32 * half + 16 * part
-            rows = wanted[start : start + 16]
+            start = 32 * half + 8 * part
+            rows = wanted[start : start + 8]
             sides.append(
                 jnp.concatenate(
-                    [rows * ones_where(row == pair) for pair in range(16)], axis=1
+                    [jnp.where(row == pair, rows, 0.0) for pair in range(8)], axis=1
                 )
             )
-        weights = flipped[16 * part : 16 * part + 16].reshape(16 * WIDE, WIDE)
-        terms = dot(jnp.concatenate(sides, axis=0), weights)
-        lower.append(terms[0:16])
-        upper.append(terms[16:32])
+        weights = flipped[8 * part : 8 * part + 8].reshape(8 * WIDE, WIDE)
+        terms = dot(jnp.concatenate(sides, axis=0).astype(bf16), weights)
+        lower.append(terms[0:8])
+        upper.append(terms[8:16])
     terms = jnp.concatenate(lower + upper, axis=0)
     wrong = (iota((ENT, WIDE), 0) < ENT // 2) == (iota((ENT, WIDE), 1) >= TALL)
     sums = dot(pick_t, split_terms(jnp.where(wrong, 0.0, terms), 3))
@@ -432,7 +432,7 @@
         id_column, mass_in, matrix_far = rest[0:3]
         payload, new_current, new_advance, new_forces, mass_rows = rest[3:8]
         share, share_t, own, matrix, slot_labels = rest[8:13]
-        spread, picked, sem = rest[13:]
+        picked, sem = rest[13:]
         copy = pltpu.make_async_copy(matrix_far, matrix, sem)
         copy.start()
         me = lax.axis_index("soil")
@@ -488,9 +488,9 @@
     else:
         forces_in, mass_in, share, share_t, own, matrix = rest[0:6]
         if is_last:
-            outputs, (spread, picked) = rest[6:-2], rest[-2:]
+            outputs, picked = rest[6:-1], rest[-1]
         else:
-            slot_column, outputs, (spread, picked) = rest[6], rest[7:-2], rest[-2:]
+            slot_column, outputs, picked = rest[6], rest[7:-1], rest[-1]
         size = 8 if is_last else 16
         tail = arrived[:, SHARE_ROWS:, :].astype(f32).reshape(size * SOIL, 128).astype(bf16)
         tail_lane = iota((3 * SOIL, size * SOIL), 1)
@@ -513,16 +513,12 @@
             chosen = [ones_where(lane == first + float(CAP * c)) for c in range(3)]
             mass_all += side_by_side(dot(jnp.concatenate(chosen, axis=0), tail), ENT)
         wanted = sums * mass_all
-    pieces = pull(wanted.astype(bf16), pick_t[...], flipped)
-
-    device = iota((SOIL, WIDE), 0)
-    for peer in range(SOIL):
-        spread[:, WIDE * peer : WIDE * peer + WIDE] = jnp.where(
-            device == peer, tire_all, 0.0
-        ).astype(bf16)
+    pieces = pull(wanted, pick_t[...], flipped)
+
+    line = jnp.concatenate([tire_all[peer : peer + 1] for peer in range(SOIL)], axis=1)
     if copy is not None:
         copy.wait()
-    tire = jnp.sum(dot(spread[...], matrix[...]), axis=0, keepdims=True)
+    tire = dot(line.astype(bf16), matrix[...])
 
     row = iota((CB, 128), 0)
     moved = []
@@ -573,16 +569,17 @@
 ):
     copies = [
         pltpu.make_async_copy(
-            tiles_far.at[pl.ds(16 * g, 16)], tiles.at[pl.ds(16 * g, 16)], sems.at[g]
-        )
-        for g in range(4)
+            tiles_far.at[pl.ds(8 * g, 8)], tiles.at[pl.ds(8 * g, 8)], sems.at[g]
+        )
+        for g in range(8)
     ]
     for copy in copies:
         copy.start()
     picked = dot(pick[...], doubles[...]).astype(bf16)
     mask = entry_mask()
     for group in range(4):
-        copies[group].wait()
+        copies[2 * group].wait()
+        copies[2 * group + 1].wait()
         part = slice(16 * group, 16 * group + 16)
         spread = jnp.concatenate([picked[part]] * 8, axis=1) * mask
         forces[part] = dot(spread, tiles[part].reshape(16 * TALL, WIDE))
@@ -625,7 +622,7 @@
 
 
 def step_scratch():
-    return [pltpu.VMEM((SOIL, SOIL * 3 * TC), bf16), pltpu.VMEM((ENT, WIDE), bf16)]
+    return [pltpu.VMEM((ENT, WIDE), bf16)]
 
 
 def on_device(
@@ -781,7 +778,7 @@
         out_specs=(VECTOR,) * 3,
         scratch_shapes=[
             pltpu.VMEM((ENT, TALL, WIDE), bf16),
-            pltpu.SemaphoreType.DMA((4,)),
+            pltpu.SemaphoreType.DMA((8,)),
         ],
         compiler_params=params(14),
         cost_estimate=pl.CostEstimate(

time: 91.4 us -> 91.3 us (level)
  no operation moved by 1% of the time
where the time goes in v2:
time: 91.3 us; the launch traced here: 91 us
  blocking collectives  61.1 us (67%)
  Pallas kernels  23.4 us (26%)
  starting transfers between devices  4.3 us (5%)
  between operations  1.32 us (1%)
    all_to_all x3, blocking collectives, on_device(): arrived = lax.all_to_all(payload, 'soil', 0, 0, tiled=True)  50.2 us
    pallas_call x3, Pallas kernels, on_device(): pl.pallas_call(functools.partial(step_kernel, weights[iteration], is_firs...  12.9 us
    all_to_all x1, blocking collectives, on_device(): arrived = lax.all_to_all(outgoing, 'soil', 0, 0, tiled=True)  10.9 us
    pallas_call x1, Pallas kernels, on_device(): pl.pallas_call(first_kernel, out_shape=(shape_of((SOIL, SEND_FIRST, 128),...  5.13 us
    pallas_call x1, Pallas kernels, on_device(): pl.pallas_call(last_push_kernel, out_shape=(shape_of((ENT, WIDE), f32), s...  4.3 us
    all_to_all x1, starting transfers between devices, on_device(): across = lax.all_to_all(squares, 'grp', 0, 0, tiled=True)  4.3 us
  transfers between devices with their start and end apart: 1, of which 1 were waited for; matrix products, arithmetic and copies ran while one was open for 0% of the time, Pallas kernels for 5%

profile of v2, /device:TPU:0, one launch (start us, length us, event | category | flops | bytes accessed | tf_op | source)
XLA Modules:
  0.0 91.0 jit_solution(11754940121838503013)
XLA Ops:
  1.3 5.1 %first.1 = (bf16[16,248,128]{2,1,0:T(8,128)(2,1)S(1)}, bf16[64,192,384]{2,1,0:T(8,128)(2,1)S(1)}, bf16[32,384,384]{2,1,0:T(8,128)(2,1)S(1)}, bf16[64,16]{1,0:T(8...) custom-call(s32[1]{0:T(128)S(6)} %copy.13.count, ...), custom_call_target="tpu_custom_call" | custom-call | tf_op jit(solution)/shard_map/first/pallas_call | solution.py:661
  6.4 24.7 %all_to_all.25.arrived = bf16[16,248,128]{2,1,0:T(8,128)(2,1)S(1)} all-to-all(bf16[16,248,128]{2,1,0:T(8,128)(2,1)S(1)} %get-tuple-element.38), channel_id=1, replica_groups=mesh['grp'=8,'soil'=16] {'soil'}, dimensions={0} | all-to-all | bytes 2031616 | tf_op jit(solution)/shard_map/all_to_all | solution.py:709
  31.2 5.5 %step0.1 = (bf16[16,112,128]{2,1,0:T(8,128)(2,1)S(1)}, f32[3,16,128]{2,1,0:T(8,128)S(1)}, f32[3,16,128]{2,1,0:T(8,128)S(1)}, f32[64,384]{1,0:T(8,128)S(1)}, f32[...) custom-call(bf16[16,248,128]{2,1,0:T(8,128)(2,1)S(1)} %all_to_all.25, ...), custom_call_target="tpu_custom_call" | custom-call | tf_op jit(solution)/shard_map/step0/pallas_call | solution.py:742
  36.7 13.0 %all_to_all.26.arrived = bf16[16,112,128]{2,1,0:T(8,128)(2,1)S(1)} all-to-all(bf16[16,112,128]{2,1,0:T(8,128)(2,1)S(1)} %get-tuple-element.48), channel_id=1, replica_groups=mesh['grp'=8,'soil'=16] {'soil'}, dimensions={0} | all-to-all | bytes 917504 | tf_op jit(solution)/shard_map/all_to_all | solution.py:709
  49.6 4.3 %step1.1 = (bf16[16,104,128]{2,1,0:T(8,128)(2,1)S(1)}, f32[3,16,128]{2,1,0:T(8,128)S(1)}, f32[3,16,128]{2,1,0:T(8,128)S(1)}, f32[64,384]{1,0:T(8,128)S(1)}, f32[64,384]{1,0:T(8,128)S(1)}) custom-call(bf16[16,112,128]{2,1,0:T(8,128)(2,1)S(1)} %all_to_all.26.arrived, bf16[64,16]{1,0:T(8,128)(2,1)S(1)} %get-tuple-element.39.pick, ...), custom_call_target="tpu_custom_call" | custom-call | tf_op jit(solution)/shard_map/step1/pallas_call | solution.py:742
  53.9 12.5 %all_to_all.27.arrived = bf16[16,104,128]{2,1,0:T(8,128)(2,1)S(1)} all-to-all(bf16[16,104,128]{2,1,0:T(8,128)(2,1)S(1)} %get-tuple-element.58), channel_id=1, replica_groups=mesh['grp'=8,'soil'=16] {'soil'}, dimensions={0} | all-to-all | bytes 851968 | tf_op jit(solution)/shard_map/all_to_all | solution.py:709
  66.4 3.1 %step2.1 = (f32[3,1024]{1,0:T(4,128)}, bf16[16,384]{1,0:T(8,128)(2,1)S(1)}, f32[8,1,128]{2,1,0:T(1,128)}) custom-call(bf16[16,104,128]{2,1,0:T(8,128)(2,1)S(1)} %all_to_all.27.arrived, bf16[64,16]{1,0:T(8,128)(2,1)S(1)} %get-tuple-element.39.pick, bf16[16,192]{1,0:T(8,128)(2,1)S(1)} %get-tuple-element.40.pick_t, ...), custom_call_target="tpu_custom_call" | custom-call | tf_op jit(solution)/shard_map/step2/pallas_call | solution.py:742
  69.5 4.3 %all-to-all-start.3 = ((f32[8,1,128]{2,1,0:T(1,128)}), f32[8,1,128]{2,1,0:T(1,128)S(1)}, u32[]{:S(2)}, u32[]{:S(2)}) async-start(f32[8,1,128]{2,1,0:T(1,128)} %get-tuple-element.69), calls=%async_computation.3 | async-start | bytes 8192 | tf_op jit(solution)/shard_map/all_to_all | solution.py:769
  73.8 4.3 %last_push.1 = (f32[64,384]{1,0:T(8,128)S(1)}, bf16[256,576]{1,0:T(8,128)(2,1)S(1)}, bf16[48,256]{1,0:T(8,128)(2,1)S(1)}) custom-call(bf16[16,384]{1,0:T(8,128)(2,1)S(1)} %get-tuple-element.64.doubles, bf16[64,16]{1,0:T(8,128)(2,1)S(1)} %get-tuple-element.39.pick, f32[8,64]{1,0:T(8,128)S(1)} %get-tuple-element.65.slot_row, ...), custom_call_target="tpu_custom_call" | custom-call | flops 10000000 | bytes 10000000 | tf_op jit(solution)/shard_map/last_push/pallas_call | solution.py:770
  78.1 0.9 all-to-all-done.3.across
  79.0 0.2 outgoing.1
  79.2 10.9 %all_to_all.28.arrived = f32[16,16,128]{2,1,0:T(8,128)S(1)} all-to-all(f32[16,16,128]{2,1,0:T(8,128)S(1)} %outgoing.1), channel_id=1, replica_groups=mesh['grp'=8,'soil'=16] {'soil'}, dimensions={0} | all-to-all | bytes 262144 | tf_op jit(solution)/shard_map/all_to_all | solution.py:797
  90.1 0.9 totals.1
Async XLA Ops:
  69.5 9.5 %all-to-all-start.3 = ((f32[8,1,128]{2,1,0:T(1,128)}), f32[8,1,128]{2,1,0:T(1,128)S(1)}, u32[]{:S(2)}, u32[]{:S(2)}) async-start(f32[8,1,128]{2,1,0:T(1,128)} %get-tuple-element.69), calls=%async_computation.3 | async-start | bytes 8192 | tf_op jit(solution)/shard_map/all_to_all | solution.py:769

commit v3 on v1

--- a/solution.py
+++ b/solution.py
@@ -245,12 +245,16 @@
             ]
         )
     ]
+    parts = ((0, 10), (10, 10), (20, 8), (28, 4))
     copies = []
-    for start in (0, 32, 8, 40, 16, 48, 24, 56):
-        part = pl.ds(start, 8)
-        copies.append(
-            pltpu.make_async_copy(tiles_far.at[part], tiles.at[part], tile_sems.at[start // 8])
-        )
+    for part, (start, size) in enumerate(parts):
+        for half in range(2):
+            entries = pl.ds(32 * half + start, size)
+            copies.append(
+                pltpu.make_async_copy(
+                    tiles_far.at[entries], tiles.at[entries], tile_sems.at[2 * part + half]
+                )
+            )
     for copy in small + copies[0 : 2 * 2]:
         copy.start()
     for copy in small[0:2]:
@@ -268,8 +272,8 @@
         copies[2 * part + 1].wait()
         for copy in copies[2 * (part + 2) : 2 * (part + 2) + 2]:
             copy.start()
-        for number in range(8):
-            near, away = 8 * part + number, 32 + 8 * part + number
+        for near in range(parts[part][0], parts[part][0] + parts[part][1]):
+            away = near + 32
             above, below = tiles[near], tiles[away]
             flipped[near] = jnp.concatenate([above, below], axis=0).T
             for entry, tile in ((near, above), (away, below)):

time: 91.4 us -> 91.3 us (level)
  no operation moved by 1% of the time
where the time goes in v3:
time: 91.3 us; the launch traced here: 91 us
  blocking collectives  61.1 us (67%)
  Pallas kernels  23.5 us (26%)
  starting transfers between devices  4.3 us (5%)
  between operations  1.32 us (1%)
    all_to_all x3, blocking collectives, on_device(): arrived = lax.all_to_all(payload, 'soil', 0, 0, tiled=True)  50.2 us
    pallas_call x3, Pallas kernels, on_device(): pl.pallas_call(functools.partial(step_kernel, weights[iteration], is_firs...  12.9 us
    all_to_all x1, blocking collectives, on_device(): arrived = lax.all_to_all(outgoing, 'soil', 0, 0, tiled=True)  10.9 us
    pallas_call x1, Pallas kernels, on_device(): pl.pallas_call(first_kernel, out_shape=(shape_of((SOIL, SEND_FIRST, 128),...  5.12 us
    pallas_call x1, Pallas kernels, on_device(): pl.pallas_call(last_push_kernel, out_shape=(shape_of((ENT, WIDE), f32), s...  4.32 us
    all_to_all x1, starting transfers between devices, on_device(): across = lax.all_to_all(squares, 'grp', 0, 0, tiled=True)  4.3 us
  transfers between devices with their start and end apart: 1, of which 1 were waited for; matrix products, arithmetic and copies ran while one was open for 0% of the time, Pallas kernels for 5%

profile of v3, /device:TPU:0, one launch (start us, length us, event | category | flops | bytes accessed | tf_op | source)
XLA Modules:
  0.0 91.0 jit_solution(17999363167051395667)
XLA Ops:
  1.3 5.1 %first.1 = (bf16[16,248,128]{2,1,0:T(8,128)(2,1)S(1)}, bf16[64,192,384]{2,1,0:T(8,128)(2,1)S(1)}, bf16[32,384,384]{2,1,0:T(8,128)(2,1)S(1)}, bf16[64,16]{1,0:T(8...) custom-call(s32[1]{0:T(128)S(6)} %copy.13.count, ...), custom_call_target="tpu_custom_call" | custom-call | tf_op jit(solution)/shard_map/first/pallas_call | solution.py:668
  6.4 24.7 %all_to_all.25.arrived = bf16[16,248,128]{2,1,0:T(8,128)(2,1)S(1)} all-to-all(bf16[16,248,128]{2,1,0:T(8,128)(2,1)S(1)} %get-tuple-element.38), channel_id=1, replica_groups=mesh['grp'=8,'soil'=16] {'soil'}, dimensions={0} | all-to-all | bytes 2031616 | tf_op jit(solution)/shard_map/all_to_all | solution.py:716
  31.1 5.5 %step0.1 = (bf16[16,112,128]{2,1,0:T(8,128)(2,1)S(1)}, f32[3,16,128]{2,1,0:T(8,128)S(1)}, f32[3,16,128]{2,1,0:T(8,128)S(1)}, f32[64,384]{1,0:T(8,128)S(1)}, f32[...) custom-call(bf16[16,248,128]{2,1,0:T(8,128)(2,1)S(1)} %all_to_all.25, ...), custom_call_target="tpu_custom_call" | custom-call | tf_op jit(solution)/shard_map/step0/pallas_call | solution.py:749
  36.7 13.0 %all_to_all.26.arrived = bf16[16,112,128]{2,1,0:T(8,128)(2,1)S(1)} all-to-all(bf16[16,112,128]{2,1,0:T(8,128)(2,1)S(1)} %get-tuple-element.48), channel_id=1, replica_groups=mesh['grp'=8,'soil'=16] {'soil'}, dimensions={0} | all-to-all | bytes 917504 | tf_op jit(solution)/shard_map/all_to_all | solution.py:716
  49.6 4.3 %step1.1 = (bf16[16,104,128]{2,1,0:T(8,128)(2,1)S(1)}, f32[3,16,128]{2,1,0:T(8,128)S(1)}, f32[3,16,128]{2,1,0:T(8,128)S(1)}, f32[64,384]{1,0:T(8,128)S(1)}, f32[64,384]{1,0:T(8,128)S(1)}) custom-call(bf16[16,112,128]{2,1,0:T(8,128)(2,1)S(1)} %all_to_all.26.arrived, bf16[64,16]{1,0:T(8,128)(2,1)S(1)} %get-tuple-element.39.pick, ...), custom_call_target="tpu_custom_call" | custom-call | tf_op jit(solution)/shard_map/step1/pallas_call | solution.py:749
  54.0 12.5 %all_to_all.27.arrived = bf16[16,104,128]{2,1,0:T(8,128)(2,1)S(1)} all-to-all(bf16[16,104,128]{2,1,0:T(8,128)(2,1)S(1)} %get-tuple-element.58), channel_id=1, replica_groups=mesh['grp'=8,'soil'=16] {'soil'}, dimensions={0} | all-to-all | bytes 851968 | tf_op jit(solution)/shard_map/all_to_all | solution.py:716
  66.4 3.1 %step2.1 = (f32[3,1024]{1,0:T(4,128)}, bf16[16,384]{1,0:T(8,128)(2,1)S(1)}, f32[8,1,128]{2,1,0:T(1,128)}) custom-call(bf16[16,104,128]{2,1,0:T(8,128)(2,1)S(1)} %all_to_all.27.arrived, bf16[64,16]{1,0:T(8,128)(2,1)S(1)} %get-tuple-element.39.pick, bf16[16,192]{1,0:T(8,128)(2,1)S(1)} %get-tuple-element.40.pick_t, ...), custom_call_target="tpu_custom_call" | custom-call | tf_op jit(solution)/shard_map/step2/pallas_call | solution.py:749
  69.5 4.3 %all-to-all-start.3 = ((f32[8,1,128]{2,1,0:T(1,128)}), f32[8,1,128]{2,1,0:T(1,128)S(1)}, u32[]{:S(2)}, u32[]{:S(2)}) async-start(f32[8,1,128]{2,1,0:T(1,128)} %get-tuple-element.69), calls=%async_computation.3 | async-start | bytes 8192 | tf_op jit(solution)/shard_map/all_to_all | solution.py:776
  73.8 4.3 %last_push.1 = (f32[64,384]{1,0:T(8,128)S(1)}, bf16[256,576]{1,0:T(8,128)(2,1)S(1)}, bf16[48,256]{1,0:T(8,128)(2,1)S(1)}) custom-call(bf16[16,384]{1,0:T(8,128)(2,1)S(1)} %get-tuple-element.64.doubles, bf16[64,16]{1,0:T(8,128)(2,1)S(1)} %get-tuple-element.39.pick, f32[8,64]{1,0:T(8,128)S(1)} %get-tuple-element.65.slot_row, ...), custom_call_target="tpu_custom_call" | custom-call | flops 10000000 | bytes 10000000 | tf_op jit(solution)/shard_map/last_push/pallas_call | solution.py:777
  78.1 0.9 all-to-all-done.3.across
  79.0 0.2 outgoing.1
  79.2 10.9 %all_to_all.28.arrived = f32[16,16,128]{2,1,0:T(8,128)S(1)} all-to-all(f32[16,16,128]{2,1,0:T(8,128)S(1)} %outgoing.1), channel_id=1, replica_groups=mesh['grp'=8,'soil'=16] {'soil'}, dimensions={0} | all-to-all | bytes 262144 | tf_op jit(solution)/shard_map/all_to_all | solution.py:804
  90.2 0.9 totals.1
Async XLA Ops:
  69.5 9.5 %all-to-all-start.3 = ((f32[8,1,128]{2,1,0:T(1,128)}), f32[8,1,128]{2,1,0:T(1,128)S(1)}, u32[]{:S(2)}, u32[]{:S(2)}) async-start(f32[8,1,128]{2,1,0:T(1,128)} %get-tuple-element.69), calls=%async_computation.3 | async-start | bytes 8192 | tf_op jit(solution)/shard_map/all_to_all | solution.py:776

commit v4 on v1

--- a/solution.py
+++ b/solution.py
@@ -467,12 +467,11 @@
         found, sums = [], []
         for c in range(3):
             start = FORCE_ROWS + NB * c
-            found.append(dot(name_pick, arrived[:, start : start + NB, :].reshape(BODIES, 128)))
-            plane = arrived[:, ENT * c : ENT * c + ENT, :].reshape(SOIL * ENT, 128)
-            sums.append(dot(match, plane))
-        mass_high = jnp.concatenate(found, axis=1)
+            found.append(arrived[:, start : start + NB, :].reshape(BODIES, 128))
+            sums.append(arrived[:, ENT * c : ENT * c + ENT, :].reshape(SOIL * ENT, 128))
+        mass_high = dot(name_pick, jnp.concatenate(found, axis=1))
         mass_rows[...] = mass_high
-        wanted = jnp.concatenate(sums, axis=1) * mass_high
+        wanted = dot(match, jnp.concatenate(sums, axis=1)) * mass_high
         match_shares(me, all_named, mine, share, share_t, own)
         slot_labels[...] = tails[6 * SOIL : 7 * SOIL]
         tail_pick = mass_slots(slot_hits(me, tails[6 * SOIL : 7 * SOIL]))
@@ -504,7 +503,7 @@
         received = [
             arrived[:, SHARED * c : SHARED * c + SHARED, :].reshape(ROWS, 128) for c in range(3)
         ]
-        sums = jnp.concatenate([dot(share_t[...], plane) for plane in received], axis=1)
+        sums = dot(share_t[...], jnp.concatenate(received, axis=1))
         sums += dot(own[...], split_terms(forces_in[...], 2))
         mass_all = mass_in[...]
         if not is_last:

time: 91.4 us -> 91.5 us (level)
  no operation moved by 1% of the time
where the time goes in v4:
time: 91.5 us; the launch traced here: 91.1 us
  blocking collectives  61.1 us (67%)
  Pallas kernels  23.6 us (26%)
  starting transfers between devices  4.3 us (5%)
  between operations  1.32 us (1%)
    all_to_all x3, blocking collectives, on_device(): arrived = lax.all_to_all(payload, 'soil', 0, 0, tiled=True)  50.2 us
    pallas_call x3, Pallas kernels, on_device(): pl.pallas_call(functools.partial(step_kernel, weights[iteration], is_firs...  13 us
    all_to_all x1, blocking collectives, on_device(): arrived = lax.all_to_all(outgoing, 'soil', 0, 0, tiled=True)  10.9 us
    pallas_call x1, Pallas kernels, on_device(): pl.pallas_call(first_kernel, out_shape=(shape_of((SOIL, SEND_FIRST, 128),...  5.13 us
    pallas_call x1, Pallas kernels, on_device(): pl.pallas_call(last_push_kernel, out_shape=(shape_of((ENT, WIDE), f32), s...  4.32 us
    all_to_all x1, starting transfers between devices, on_device(): across = lax.all_to_all(squares, 'grp', 0, 0, tiled=True)  4.3 us
  transfers between devices with their start and end apart: 1, of which 1 were waited for; matrix products, arithmetic and copies ran while one was open for 0% of the time, Pallas kernels for 5%

profile of v4, /device:TPU:0, one launch (start us, length us, event | category | flops | bytes accessed | tf_op | source)
XLA Modules:
  0.0 91.1 jit_solution(2450139781797085731)
XLA Ops:
  1.3 5.1 %first.1 = (bf16[16,248,128]{2,1,0:T(8,128)(2,1)S(1)}, bf16[64,192,384]{2,1,0:T(8,128)(2,1)S(1)}, bf16[32,384,384]{2,1,0:T(8,128)(2,1)S(1)}, bf16[64,16]{1,0:T(8...) custom-call(s32[1]{0:T(128)S(6)} %copy.13.count, ...), custom_call_target="tpu_custom_call" | custom-call | tf_op jit(solution)/shard_map/first/pallas_call | solution.py:663
  6.4 24.7 %all_to_all.25.arrived = bf16[16,248,128]{2,1,0:T(8,128)(2,1)S(1)} all-to-all(bf16[16,248,128]{2,1,0:T(8,128)(2,1)S(1)} %get-tuple-element.38), channel_id=1, replica_groups=mesh['grp'=8,'soil'=16] {'soil'}, dimensions={0} | all-to-all | bytes 2031616 | tf_op jit(solution)/shard_map/all_to_all | solution.py:711
  31.2 5.6 %step0.1 = (bf16[16,112,128]{2,1,0:T(8,128)(2,1)S(1)}, f32[3,16,128]{2,1,0:T(8,128)S(1)}, f32[3,16,128]{2,1,0:T(8,128)S(1)}, f32[64,384]{1,0:T(8,128)S(1)}, f32[...) custom-call(bf16[16,248,128]{2,1,0:T(8,128)(2,1)S(1)} %all_to_all.25, ...), custom_call_target="tpu_custom_call" | custom-call | tf_op jit(solution)/shard_map/step0/pallas_call | solution.py:744
  36.7 13.0 %all_to_all.26.arrived = bf16[16,112,128]{2,1,0:T(8,128)(2,1)S(1)} all-to-all(bf16[16,112,128]{2,1,0:T(8,128)(2,1)S(1)} %get-tuple-element.48), channel_id=1, replica_groups=mesh['grp'=8,'soil'=16] {'soil'}, dimensions={0} | all-to-all | bytes 917504 | tf_op jit(solution)/shard_map/all_to_all | solution.py:711
  49.7 4.3 %step1.1 = (bf16[16,104,128]{2,1,0:T(8,128)(2,1)S(1)}, f32[3,16,128]{2,1,0:T(8,128)S(1)}, f32[3,16,128]{2,1,0:T(8,128)S(1)}, f32[64,384]{1,0:T(8,128)S(1)}, f32[64,384]{1,0:T(8,128)S(1)}) custom-call(bf16[16,112,128]{2,1,0:T(8,128)(2,1)S(1)} %all_to_all.26.arrived, bf16[64,16]{1,0:T(8,128)(2,1)S(1)} %get-tuple-element.39.pick, ...), custom_call_target="tpu_custom_call" | custom-call | tf_op jit(solution)/shard_map/step1/pallas_call | solution.py:744
  54.0 12.5 %all_to_all.27.arrived = bf16[16,104,128]{2,1,0:T(8,128)(2,1)S(1)} all-to-all(bf16[16,104,128]{2,1,0:T(8,128)(2,1)S(1)} %get-tuple-element.58), channel_id=1, replica_groups=mesh['grp'=8,'soil'=16] {'soil'}, dimensions={0} | all-to-all | bytes 851968 | tf_op jit(solution)/shard_map/all_to_all | solution.py:711
  66.5 3.1 %step2.1 = (f32[3,1024]{1,0:T(4,128)}, bf16[16,384]{1,0:T(8,128)(2,1)S(1)}, f32[8,1,128]{2,1,0:T(1,128)}) custom-call(bf16[16,104,128]{2,1,0:T(8,128)(2,1)S(1)} %all_to_all.27.arrived, bf16[64,16]{1,0:T(8,128)(2,1)S(1)} %get-tuple-element.39.pick, bf16[16,192]{1,0:T(8,128)(2,1)S(1)} %get-tuple-element.40.pick_t, ...), custom_call_target="tpu_custom_call" | custom-call | tf_op jit(solution)/shard_map/step2/pallas_call | solution.py:744
  69.6 4.3 %all-to-all-start.3 = ((f32[8,1,128]{2,1,0:T(1,128)}), f32[8,1,128]{2,1,0:T(1,128)S(1)}, u32[]{:S(2)}, u32[]{:S(2)}) async-start(f32[8,1,128]{2,1,0:T(1,128)} %get-tuple-element.69), calls=%async_computation.3 | async-start | bytes 8192 | tf_op jit(solution)/shard_map/all_to_all | solution.py:771
  73.9 4.3 %last_push.1 = (f32[64,384]{1,0:T(8,128)S(1)}, bf16[256,576]{1,0:T(8,128)(2,1)S(1)}, bf16[48,256]{1,0:T(8,128)(2,1)S(1)}) custom-call(bf16[16,384]{1,0:T(8,128)(2,1)S(1)} %get-tuple-element.64.doubles, bf16[64,16]{1,0:T(8,128)(2,1)S(1)} %get-tuple-element.39.pick, f32[8,64]{1,0:T(8,128)S(1)} %get-tuple-element.65.slot_row, ...), custom_call_target="tpu_custom_call" | custom-call | flops 10000000 | bytes 10000000 | tf_op jit(solution)/shard_map/last_push/pallas_call | solution.py:772
  78.2 0.9 all-to-all-done.3.across
  79.1 0.2 outgoing.1
  79.3 10.9 %all_to_all.28.arrived = f32[16,16,128]{2,1,0:T(8,128)S(1)} all-to-all(f32[16,16,128]{2,1,0:T(8,128)S(1)} %outgoing.1), channel_id=1, replica_groups=mesh['grp'=8,'soil'=16] {'soil'}, dimensions={0} | all-to-all | bytes 262144 | tf_op jit(solution)/shard_map/all_to_all | solution.py:799
  90.3 0.9 totals.1
Async XLA Ops:
  69.6 9.5 %all-to-all-start.3 = ((f32[8,1,128]{2,1,0:T(1,128)}), f32[8,1,128]{2,1,0:T(1,128)S(1)}, u32[]{:S(2)}, u32[]{:S(2)}) async-start(f32[8,1,128]{2,1,0:T(1,128)} %get-tuple-element.69), calls=%async_computation.3 | async-start | bytes 8192 | tf_op jit(solution)/shard_map/all_to_all | solution.py:771
